TPU v7x, 512 devices: a whole 4x4x16 slice. The times are simulated.
512 devices in a mesh: group: 4 (over z_hi), dp: 32 (over y, z_lo, core), tensor: 4 (over x).
Axes of the slice: x: 4, y: 4, z: 16 (z_hi: 4, z_lo: 4; z = z_hi * 4 + z_lo), core: 2. Of those that a mesh axis runs over, the one named last changes fastest.
Arguments:
- queries: bfloat16 [16384, 4096], P(('group', 'dp'), 'tensor'), may hold values from -16 to 16
- span_state: bfloat16 [16384, 4096], P(('group', 'dp'), 'tensor'), may hold values from -6 to 6
- neigh_state: bfloat16 [65536, 4096], P(('group', 'dp'), 'tensor'), may hold values from -24 to 24
- counts: int32 [4, 64], P('group'), may hold values from 1 to 2
- norm_gain: float32 [4096], P('tensor'), may hold values from 0.5 to 1.5
- head_gate: float32 [32], P('tensor'), may hold values from 0.3 to 1.5
- out_grad: bfloat16 [16384, 4096], P(('group', 'dp'), 'tensor'), may hold values from -6 to 6
Outputs:
- cross_output: bfloat16 [16384, 4096], P(('group', 'dp'), 'tensor')
- query_grad: bfloat16 [16384, 4096], P(('group', 'dp'), 'tensor')
- span_grad: bfloat16 [16384, 4096], P(('group', 'dp'), 'tensor')
- neighbour_grad: bfloat16 [65536, 4096], P(('group', 'dp'), 'tensor')
- gate_grad: float32 [32], P('tensor')
Inputs may be any that keep to these rules, and one draw needn't show every extreme that they name: Slot j of span c holds a retrieved neighbour exactly when j < counts[c].
All inputs are finite; a program needn't handle non-finite values.
Results may differ from a plain program's by a relative error of at most 0.0095.
The roundings to bfloat16 on the way count: a program that leaves them out, or rounds other values in their place, can miss the bound.
Values may be sent and summed in bfloat16 or wider, within the bound.
No kernel may reach another device: no remote copies, remote signals or barrier semaphores. Data moves between devices by JAX's collectives and lax.ppermute only.
A program may use at most 64 MiB of HBM per device.

v0:
```python
import math
import jax
import jax.numpy as jnp
from jax import lax
from jax.sharding import PartitionSpec as P

CH = 64
NB = 2
NL = 128
epsilon = 1e-05
masked_score = -1e30


def shifted(value, axis, steps):
    count = lax.axis_size(axis)
    leading, last = (max(0, -steps), min(count, count - steps))
    return lax.ppermute(value, axis, [(source, source + steps) for source in range(leading, last)])


def product(form, left, right):
    return jnp.einsum(form, left, right, preferred_element_type=jnp.float32)


def encoder_forward(normed, neighbours, contexts):
    slot_count = normed.shape[1]
    spread = jnp.broadcast_to(
        contexts[:, None], (contexts.shape[0], slot_count) + contexts.shape[1:]
    )
    all_keys = jnp.concatenate([normed, spread], axis=2)
    scores = product("cjqhd,cjkhd->cjhqk", normed, all_keys) / normed.shape[-1]
    powers = jnp.exp(scores)
    weights = powers / jnp.sum(powers, axis=-1, keepdims=True)
    rounded = weights.astype(jnp.bfloat16)
    mixture = product("cjhqk,cjkhd->cjqhd", rounded, all_keys)
    encoded = (neighbours.astype(jnp.float32) + mixture).astype(jnp.bfloat16)
    return (encoded, (all_keys, weights, rounded, mixture))


def encoder_backward(grad_encoded, normed, saved):
    all_keys, weights, rounded, mixture = saved
    grad_rounded = grad_encoded.astype(jnp.bfloat16)
    grad_weights = product("cjqhd,cjkhd->cjhqk", grad_rounded, all_keys)
    offset = jnp.moveaxis(jnp.sum(grad_encoded * mixture, axis=-1), -1, 2)[..., None]
    score_grad = (weights * (grad_weights - offset) / normed.shape[-1]).astype(jnp.bfloat16)
    normed_grad = product("cjhqk,cjkhd->cjqhd", score_grad, all_keys)
    key_grad = product("cjhqk,cjqhd->cjkhd", score_grad, normed) + product(
        "cjhqk,cjqhd->cjkhd", rounded, grad_rounded
    )
    length = normed.shape[2]
    normed_grad = normed_grad + key_grad[:, :, :length]
    context_grad = jnp.sum(key_grad[:, :, length:], axis=1)
    return (normed_grad, context_grad)


def cross_attend(blocks, grad_blocks, keys, usable, present, gate_tanh):
    scale = 1.0 / math.sqrt(blocks.shape[-1])
    scores = product("brhd,bmhd->bhrm", blocks, keys) * scale
    scores = jnp.where(usable[:, None, None, :], scores, masked_score)
    highest = jnp.max(scores, axis=-1, keepdims=True)
    powers = jnp.exp(scores - highest)
    weights = powers / jnp.sum(powers, axis=-1, keepdims=True)
    rounded = weights.astype(jnp.bfloat16)
    attended = product("bhrm,bmhd->brhd", rounded, keys)
    present_mask = present[:, None, None, None]
    attended = jnp.where(present_mask, attended, 0.0)
    output = (gate_tanh[:, None] * attended).astype(jnp.bfloat16)
    grad_output = grad_blocks.astype(jnp.float32)
    gate_term = jnp.sum(grad_output * attended, axis=(0, 1, 3))
    att_grad = jnp.where(present_mask, gate_tanh[:, None] * grad_output, 0.0)
    grad_rounded = att_grad.astype(jnp.bfloat16)
    grad_weights = product("brhd,bmhd->bhrm", grad_rounded, keys)
    offset = jnp.moveaxis(jnp.sum(att_grad * attended, axis=-1), -1, 1)[..., None]
    score_grad = (weights * (grad_weights - offset) * scale).astype(jnp.bfloat16)
    query_grad = product("bhrm,bmhd->brhd", score_grad, keys).astype(jnp.bfloat16)
    key_grad = product("bhrm,brhd->bmhd", score_grad, blocks) + product(
        "bhrm,brhd->bmhd", rounded, grad_rounded
    )
    return (output, query_grad, key_grad, gate_term)


def shards(queries, span_state, neigh_state, counts, norm_gain, head_gate, out_grad):
    head_count = head_gate.shape[0]
    local_width = queries.shape[1]
    head_dim = local_width // head_count
    row_count = queries.shape[0]
    span_count = row_count // CH
    seq_spans = counts.shape[1]
    lead = CH - 1

    def blockify(matrix):
        return matrix.reshape(-1, CH, head_count, head_dim)

    neighbours = neigh_state.reshape(span_count, NB, NL, head_count, head_dim)
    contexts = span_state.reshape(span_count, CH, head_count, head_dim)
    gains = norm_gain.reshape(head_count, head_dim)
    floats = neighbours.astype(jnp.float32)
    square_sum = lax.psum(jnp.sum(floats * floats, axis=(3, 4)), "tensor")
    full_width = lax.axis_size("tensor") * local_width
    inverse = lax.rsqrt(square_sum / full_width + epsilon)[..., None, None]
    scaled = floats * inverse
    normed = (scaled * gains).astype(jnp.bfloat16)
    encoded, saved = encoder_forward(normed, neighbours, contexts)
    line_index = lax.axis_index("dp")
    first_span = line_index * span_count
    flat_counts = counts.reshape(-1)
    own_counts = lax.dynamic_slice_in_dim(flat_counts, first_span, span_count)
    gate_tanh = jnp.tanh(head_gate)
    usable = jnp.repeat(jnp.arange(NB)[None, :] < own_counts[:, None], NL, axis=1)
    present = own_counts > 0
    keys = encoded.reshape(span_count, NB * NL, head_count, head_dim)
    kept = row_count - lead
    padding = jnp.zeros((lead, local_width), jnp.bfloat16)
    blocks = blockify(jnp.concatenate([queries[lead:], padding], axis=0))
    grad_blocks = blockify(jnp.concatenate([out_grad[lead:], padding], axis=0))
    earlier_keys = shifted(keys[span_count - 1], "dp", 1)
    earlier_count = lax.dynamic_index_in_dim(
        flat_counts, jnp.maximum(first_span - 1, 0), keepdims=False
    )
    earlier_present = jnp.logical_and(first_span % seq_spans > 0, earlier_count > 0)
    earlier_usable = jnp.repeat(jnp.arange(NB) < earlier_count, NL)
    front_row = jnp.zeros((1, local_width), jnp.bfloat16)
    first_block = blockify(jnp.concatenate([front_row, queries[:lead]], axis=0))
    first_grad = blockify(jnp.concatenate([front_row, out_grad[:lead]], axis=0))
    front_out, front_query, front_keys, front_term = cross_attend(
        first_block,
        first_grad,
        earlier_keys[None],
        earlier_usable[None],
        earlier_present[None],
        gate_tanh,
    )
    local_out, local_query, key_grad, local_term = cross_attend(
        blocks, grad_blocks, keys, usable, present, gate_tanh
    )
    returned = shifted(front_keys[0].astype(jnp.bfloat16), "dp", -1).astype(jnp.float32)
    key_grad = key_grad.at[span_count - 1].add(returned)
    cross_output = jnp.concatenate(
        [front_out.reshape(CH, local_width)[1:], local_out.reshape(row_count, local_width)[:kept]],
        axis=0,
    )
    query_grad = jnp.concatenate(
        [
            front_query.reshape(CH, local_width)[1:],
            local_query.reshape(row_count, local_width)[:kept],
        ],
        axis=0,
    )
    gate_terms = front_term + local_term
    grad_encoded = key_grad.reshape(span_count, NB, NL, head_count, head_dim)
    normed_grad, context_grad = encoder_backward(grad_encoded, normed, saved)
    gain_grad = normed_grad * gains
    projection = lax.psum(jnp.sum(gain_grad * scaled, axis=(3, 4)), "tensor") / full_width
    neighbour_grad = grad_encoded + inverse * (gain_grad - scaled * projection[..., None, None])
    total_tokens = lax.axis_size("group") * lax.axis_size("dp") * row_count
    summed = lax.psum(gate_terms, ("group", "dp"))
    gate_grad = (1.0 - gate_tanh * gate_tanh) * summed / math.sqrt(total_tokens)
    return (
        cross_output,
        query_grad,
        context_grad.reshape(row_count, local_width).astype(jnp.bfloat16),
        neighbour_grad.reshape(-1, local_width).astype(jnp.bfloat16),
        gate_grad,
    )


def solution(mesh):
    return jax.shard_map(
        shards,
        mesh=mesh,
        in_specs=(
            P(("group", "dp"), "tensor"),
            P(("group", "dp"), "tensor"),
            P(("group", "dp"), "tensor"),
            P("group", None),
            P("tensor"),
            P("tensor"),
            P(("group", "dp"), "tensor"),
        ),
        out_specs=(
            P(("group", "dp"), "tensor"),
            P(("group", "dp"), "tensor"),
            P(("group", "dp"), "tensor"),
            P(("group", "dp"), "tensor"),
            P("tensor"),
        ),
        check_vma=False,
    )
```

profile of v0, /device:TPU:2, one launch (start us, length us, event | category | flops | bytes accessed | tf_op | source)
XLA Modules:
  0.0 361.5 jit_solution(13486729681499176493)
XLA Ops:
  0.6 1.5 fusion.4
  2.2 2.8 convert_bitcast_fusion
  5.0 13.6 %psum.21 = f32[2,2,128]{2,1,0:T(2,128)S(1)} all-reduce(f32[2,2,128]{2,1,0:T(2,128)S(1)} %bitcast.184), channel_id=1, replica_groups=mesh['group'=4,'dp'=32,'tensor'=4] {'tensor'}, use_global_device_ids=true, to_apply=%region_1.0 | all-reduce | flops 512 | bytes 4096 | tf_op jit(solution)/shard_map/psum | solution.py:97
  18.7 2.1 copy.109
  20.8 0.5 multiply_convert_fusion.1
  21.4 0.1 broadcast_in_dim.103
  21.5 0.8 fusion.3
  22.4 0.1 copy-done.5
  22.5 2.4 fusion.6
  25.0 0.9 copy-done.4
  25.9 0.3 copy.78
  26.3 0.9 copy.79
  27.2 2.1 collective-permute-start
  29.3 0.6 constant_dynamic-slice_fusion.1
  30.5 1.2 iota_compare_fusion.1
  31.8 0.7 slice.76
  32.5 1.9 copy.82
  34.5 0.5 tanh.3
  35.0 0.6 broadcast_compare_fusion
  35.7 0.1 broadcast_bitcast_fusion
  35.8 0.9 convert_bitcast_fusion.1
  36.8 0.9 copy.117
  37.7 0.5 fusion.12
  38.2 1.0 copy-done.3
  39.2 1.2 fusion.66
  40.4 5.0 %multiply_reduce_fusion.1 = (f32[8]{0:T(128)}, f32[2,64,8]{1,2,0:T(8,128)}, bf16[2,64,8,128]{3,1,2,0:T(8,128)(2,1)}) fusion(f32[2,64,8,128]{3,2,1,0:T(8,128)} %bitcast.171, f32[8]{0:T(128)} %tanh.3, pred[2]{0:T(512)(128)(4,1)} %get-tuple-element.21, bf16[2,256,8,128]{3,2,1,0:T(8,128)(2,1)S(1)} %bitcast.155, f32[2,8,64]{2,1,0:T(8,128)S(1)} %get-tuple-element.30, ...), kind=kOutput, calls=%fused_computation.63 | convolution fusion | flops 69075192 | bytes 2891842 | tf_op jit(solution)/shard_map/bhrm,bmhd->brhd/dot_general | solution.py:21
  45.4 2.0 fusion.13
  47.4 1.0 fusion.26
  48.4 1.9 fusion.41
  50.3 0.8 convert_bitcast_fusion.3
  51.1 0.8 copy.115
  51.9 0.2 copy.93
  52.1 0.2 copy.86
  52.4 0.1 broadcast_bitcast_fusion.1
  52.5 6.2 %add_bitcast_fusion.1 = f32[2,256,8,128]{1,3,2,0:T(8,128)} fusion(f32[2,8,128,256]{3,2,1,0:T(8,128)} %fusion.41, f32[2,64,8,128]{3,2,1,0:T(8,128)} %bitcast.173, f32[8]{0:T(128)S(1)} %copy-done.14, pred[2]{0:T(512)(128)(4,1)S(1)} %copy-done.16, f32[2,8,64]{2,1,0:T(8,128)S(1)} %get-tuple-element.30, f32[2,8,64,256]{3,2,1,0:T(8,128)} %copy-done.3), kind=kOutput, calls=%fused_computation.18 | convolution fusion | flops 68814080 | bytes 5771298 | tf_op jit(solution)/shard_map/bhrm,brhd->bmhd/dot_general | solution.py:21
  58.6 1.4 fusion.21
  60.0 0.9 fusion.67
  60.9 2.8 multiply_reduce_fusion.3
  63.7 1.6 fusion.24
  65.3 1.3 fusion.45
  66.7 3.4 fusion.17
  70.1 1.3 collective-permute-start.1
  71.4 1.0 fusion.40
  72.4 254.7 %psum.23 = f32[8]{0:T(128)S(1)} all-reduce(f32[8]{0:T(128)S(1)} %add.79), channel_id=1, replica_groups=mesh['group'=4,'dp'=32,'tensor'=4] {'group','dp'}, use_global_device_ids=true, to_apply=%region_15.16 | all-reduce | flops 8 | bytes 64 | tf_op jit(solution)/shard_map/psum | solution.py:155
  327.2 0.1 copy.182
  327.3 1.3 fusion.27
  328.6 0.1 copy.181
  328.8 0.9 pad_maximum_fusion.5
  329.6 0.5 multiply_multiply_fusion
  330.2 2.3 fusion.28
  332.5 3.0 copy.96
  335.5 1.9 convert_element_type.156
  337.4 0.3 copy-done
  337.7 2.3 fusion.7
  340.1 1.2 multiply_convert_fusion
  341.3 0.6 fusion.68
  341.9 0.9 add_bitcast_fusion
  342.8 2.6 multiply_reduce_fusion
  345.4 0.2 copy.100
  345.6 0.8 copy.178
  346.3 10.1 %psum.22 = f32[2,2,128]{2,1,0:T(2,128)S(1)} all-reduce(f32[2,2,128]{2,1,0:T(2,128)S(1)} %get-tuple-element.35), channel_id=1, replica_groups=mesh['group'=4,'dp'=32,'tensor'=4] {'tensor'}, use_global_device_ids=true, to_apply=%region_12.13 | all-reduce | flops 512 | bytes 4096 | tf_op jit(solution)/shard_map/psum | solution.py:152
  356.5 3.1 add_convert_fusion
  359.6 0.7 copy.103
  360.3 1.3 copy.177
  (72 shorter events, 0.7 us)
Async XLA Ops:
  0.6 18.0 %copy-start.10 = (bf16[128,1024]{1,0:T(8,128)(2,1)S(1)}, bf16[128,1024]{1,0:T(8,128)(2,1)}, u32[]{:S(2)}) copy-start(bf16[128,1024]{1,0:T(8,128)(2,1)} %param.10) | copy-start | bytes 786436
  18.7 2.1 copy-start.13
  21.4 1.0 copy-start.1
  21.5 1.0 copy-start.5
  22.4 2.6 copy-start.21
  22.4 2.6 copy-start.23
  24.9 1.0 copy-start.4
  24.9 4.4 %copy-start.15 = (s32[1,64]{1,0:T(1,128)S(1)}, s32[1,64]{1,0:T(1,128)}, u32[]{:S(2)}) copy-start(s32[1,64]{1,0:T(1,128)} %param.12) | copy-start | bytes 772
  24.9 6.8 %copy-start.9 = (bf16[128,1024]{1,0:T(8,128)(2,1)S(1)}, bf16[128,1024]{1,0:T(8,128)(2,1)}, u32[]{:S(2)}) copy-start(bf16[128,1024]{1,0:T(8,128)(2,1)} %param.9) | copy-start | bytes 786436
  25.0 6.9 %copy-start.8 = (bf16[128,1024]{1,0:T(8,128)(2,1)S(1)}, bf16[128,1024]{1,0:T(8,128)(2,1)}, u32[]{:S(2)}) copy-start(bf16[128,1024]{1,0:T(8,128)(2,1)} %param.15) | copy-start | bytes 786436
  26.3 8.2 %copy-start.17 = (f32[8]{0:T(128)S(1)}, f32[8]{0:T(128)}, u32[]{:S(2)}) copy-start(f32[8]{0:T(128)} %param.14) | copy-start | bytes 100
  27.2 31.4 %collective-permute-start = (bf16[256,8,128]{2,0,1:T(8,128)(2,1)}, bf16[256,8,128]{2,0,1:T(8,128)(2,1)}, u32[]{:S(2)}, u32[]{:S(2)}) collective-permute-start(bf16[256,8,128]{2,0,1:T(8,128)(2,1)} %copy.79), channel_id=1, source_target_pairs={{0,4},{4,8},{8,12},{12,16},{16,20},{20,24},{24,28},{28,32},{32,36}... | collective-permute-start | bytes 1572872 | tf_op jit(solution)/shard_map/ppermute | solution.py:17
  38.2 1.0 copy-start.3
  48.4 1.9 slice-start
  48.4 3.4 copy-start.7
  50.3 1.8 copy-start.12
  50.3 2.1 copy-start.20
  50.3 2.1 copy-start.14
  50.3 2.1 copy-start.16
  58.6 2.3 copy-start.11
  65.3 6.0 %copy-start.19 = (f32[8]{0:T(128)S(1)}, f32[8]{0:T(128)}, u32[]{:S(2)}) copy-start(f32[8]{0:T(128)} %get-tuple-element.17) | copy-start | bytes 100
  70.1 260.1 %collective-permute-start.1 = (bf16[256,8,128]{0,2,1:T(8,128)(2,1)}, bf16[256,8,128]{0,2,1:T(8,128)(2,1)S(1)}, u32[]{:S(2)}, u32[]{:S(2)}) collective-permute-start(bf16[256,8,128]{0,2,1:T(8,128)(2,1)} %fusion.17), channel_id=1, source_target_pairs={{4,0},{8,4},{12,8},{16,12},{20,16},{24,20},{28,24},{32,28},{36,32}... | collective-permute-start | bytes 1572872 | tf_op jit(solution)/shard_map/ppermute | solution.py:17
  71.4 258.3 %copy-start.18 = (f32[8]{0:T(128)S(1)}, f32[8]{0:T(128)}, u32[]{:S(2)}) copy-start(f32[8]{0:T(128)} %param.14) | copy-start | bytes 100
  335.5 2.2 copy-start
  335.5 4.6 %copy-start.22 = (f32[2,2,8,128,192]{3,4,2,1,0:T(8,128)S(1)}, f32[2,2,8,128,192]{3,4,2,1,0:T(8,128)}, u32[]{:S(2)}) copy-start(f32[2,2,8,128,192]{3,4,2,1,0:T(8,128)} %copy-done.21) | copy-start | bytes 9437188
  337.7 2.3 copy-start.2
  337.7 2.4 copy-start.6
  337.7 2.4 copy-start.24
where the time goes:
time: 362 us
  blocking collectives  278 us (77%)
  matrix products  36.8 us (10%)
  other arithmetic  22.9 us (6%)
  local copies, waits for them, and re-layouts  18.3 us (5%)
    psum x1, blocking collectives, shards(): summed = lax.psum(gate_terms, ('group', 'dp'))  255 us
    dot_general x18, matrix products, product(): return jnp.einsum(form, left, right, preferred_element_type=jnp.float32)  36.8 us
    psum x1, blocking collectives, shards(): square_sum = lax.psum(jnp.sum(floats * floats, axis=(3, 4)), 'tensor')  13.6 us
    psum x1, blocking collectives, shards(): lax.psum(jnp.sum(gain_grad * scaled, axis=(3, 4)), 'tensor') / full_width  10.1 us
    unnamed x66, local copies, waits for them, and re-layouts  8.57 us
  transfers between devices with their start and end apart: 2, of which 0 were waited for; matrix products, arithmetic and copies ran while one was open for 9% of the time, Pallas kernels for 0%

commit v1 on v0

--- a/solution.py
+++ b/solution.py
@@ -152,7 +152,7 @@
     projection = lax.psum(jnp.sum(gain_grad * scaled, axis=(3, 4)), "tensor") / full_width
     neighbour_grad = grad_encoded + inverse * (gain_grad - scaled * projection[..., None, None])
     total_tokens = lax.axis_size("group") * lax.axis_size("dp") * row_count
-    summed = lax.psum(gate_terms, ("group", "dp"))
+    summed = lax.psum(lax.psum(gate_terms, "group"), "dp")
     gate_grad = (1.0 - gate_tanh * gate_tanh) * summed / math.sqrt(total_tokens)
     return (
         cross_output,

time: 362 us -> 195 us (0.54)
  blocking collectives: 278 us -> 111 us
    psum x1 -> x2, blocking collectives: 255 us -> 87.1 us  [shards(): summed = lax.psum(lax.psum(gate_terms, 'group'), 'dp')]
  transfers between devices with their start and end apart: 2 -> 2, of which waited for: 0 -> 0; matrix products, arithmetic and copies ran while one was open for 9% -> 16% of each run, Pallas kernels for 0% -> 0%
where the time goes in v1:
time: 195 us; the launch traced here: 194 us
  blocking collectives  111 us (57%)
  matrix products  36.8 us (19%)
  other arithmetic  22.9 us (12%)
  local copies, waits for them, and re-layouts  18.3 us (9%)
  starting transfers between devices  3.38 us (2%)
    psum x2, blocking collectives, shards(): summed = lax.psum(lax.psum(gate_terms, 'group'), 'dp')  87.1 us
    dot_general x18, matrix products, product(): return jnp.einsum(form, left, right, preferred_element_type=jnp.float32)  36.8 us
    psum x1, blocking collectives, shards(): square_sum = lax.psum(jnp.sum(floats * floats, axis=(3, 4)), 'tensor')  13.6 us
    psum x1, blocking collectives, shards(): lax.psum(jnp.sum(gain_grad * scaled, axis=(3, 4)), 'tensor') / full_width  10.1 us
    unnamed x66, local copies, waits for them, and re-layouts  8.56 us
    unnamed x3, other arithmetic  4.53 us
  transfers between devices with their start and end apart: 2, of which 0 were waited for; matrix products, arithmetic and copies ran while one was open for 16% of the time, Pallas kernels for 0%

profile of v1, /device:TPU:2, one launch (start us, length us, event | category | flops | bytes accessed | tf_op | source)
XLA Modules:
  0.0 193.9 jit_solution(5156861810261073541)
XLA Ops:
  0.6 1.5 fusion.4
  2.2 2.8 %convert_bitcast_fusion = f32[64,8,8,128]{3,1,2,0:T(8,128)} fusion(bf16[512,1024]{1,0:T(8,128)(2,1)} %param.11), kind=kLoop, calls=%fused_computation.8 | loop fusion | flops 524288 | bytes 3145728
  5.0 13.6 %psum.28 = f32[2,2,128]{2,1,0:T(2,128)S(1)} all-reduce(f32[2,2,128]{2,1,0:T(2,128)S(1)} %bitcast.184), channel_id=1, replica_groups=mesh['group'=4,'dp'=32,'tensor'=4] {'tensor'}, use_global_device_ids=true, to_apply=%region_1.0 | all-reduce | flops 512 | bytes 4096 | tf_op jit(solution)/shard_map/psum | solution.py:97
  18.7 2.1 %copy.109 = f32[64,8,8,128]{3,2,1,0:T(8,128)S(1)} copy(f32[64,8,8,128]{3,1,2,0:T(8,128)} %convert_bitcast_fusion) | data formatting | bytes 4194304
  20.8 0.5 multiply_convert_fusion.1
  21.4 0.1 broadcast_in_dim.103
  21.5 0.8 fusion.3
  22.4 0.1 copy-done.5
  22.5 2.4 %fusion.6 = (bf16[2,2,128,8,128]{4,2,3,1,0:T(8,128)(2,1)S(1)}, f32[2,2,8,128,128]{3,4,2,1,0:T(8,128)}) fusion(f32[2,2,128,8,128]{4,3,2,1,0:T(8,128)S(1)} %bitcast.148, f32[2,2,8,128]{3,2,1,0:T(8,128)S(1)} %get-tuple-element.26, f32[2,2,8,128,192]{3,4,2,1,0:T(8,128)S(1)} %get-tuple-element.27, bf16[2,2,64,8,128]{4,2,3,1,0:T(8,128)(2,1)S(1)} %broadcast_in_dim.103, ...), kind=kOutput, calls=%fused_computation.14 | convolution fusion | flops 207880192 | bytes 9977856 | tf_op jit(solution)/shard_map/cjhqk,cjkhd->cjqhd/dot_general | solution.py:21
  25.0 0.9 copy-done.4
  25.9 0.3 copy.78
  26.3 0.9 copy.79
  27.2 2.1 %collective-permute-start = (bf16[256,8,128]{2,0,1:T(8,128)(2,1)}, bf16[256,8,128]{2,0,1:T(8,128)(2,1)}, u32[]{:S(2)}, u32[]{:S(2)}) collective-permute-start(bf16[256,8,128]{2,0,1:T(8,128)(2,1)} %copy.79), channel_id=1, source_target_pairs={{0,4},{4,8},{8,12},{12,16},{16,20},{20,24},{24,28},{28,32},{32,36}... | collective-permute-start | bytes 1572872 | tf_op jit(solution)/shard_map/ppermute | solution.py:17
  29.3 0.6 constant_dynamic-slice_fusion.1
  30.5 1.2 iota_compare_fusion.1
  31.8 0.7 slice.76
  32.5 1.9 copy.82
  34.5 0.5 tanh.3
  35.0 0.6 broadcast_compare_fusion
  35.7 0.1 broadcast_bitcast_fusion
  35.8 0.9 convert_bitcast_fusion.1
  36.8 0.9 copy.117
  37.7 0.5 fusion.12
  38.2 1.0 copy-done.3
  39.2 1.2 fusion.66
  40.4 5.0 %multiply_reduce_fusion.1 = (f32[8]{0:T(128)}, f32[2,64,8]{1,2,0:T(8,128)}, bf16[2,64,8,128]{3,1,2,0:T(8,128)(2,1)}) fusion(f32[2,64,8,128]{3,2,1,0:T(8,128)} %bitcast.171, f32[8]{0:T(128)} %tanh.3, pred[2]{0:T(512)(128)(4,1)} %get-tuple-element.21, bf16[2,256,8,128]{3,2,1,0:T(8,128)(2,1)S(1)} %bitcast.155, f32[2,8,64]{2,1,0:T(8,128)S(1)} %get-tuple-element.30, ...), kind=kOutput, calls=%fused_computation.63 | convolution fusion | flops 69075192 | bytes 2891842 | tf_op jit(solution)/shard_map/bhrm,bmhd->brhd/dot_general | solution.py:21
  45.4 2.0 %fusion.13 = bf16[2,8,64,256]{3,2,1,0:T(8,128)(2,1)S(1)} fusion(bf16[2,256,8,128]{3,2,1,0:T(8,128)(2,1)S(1)} %bitcast.156, f32[2,8,64]{2,1,0:T(8,128)} %bitcast.186, f32[2,8,64,256]{3,2,1,0:T(8,128)} %get-tuple-element.31, f32[2,8,64]{2,1,0:T(8,128)S(1)} %get-tuple-element.30, f32[2,64,8,128]{3,2,1,0:T(8,128)} %bitcast.172, f32[8]{0:T(128)} %tanh.3, ...), kind=kOutput, calls=%fused_computation.30 | convolution fusion | flops 68812800 | bytes 3153954 | tf_op jit(solution)/shard_map/brhd,bmhd->bhrm/dot_general | solution.py:21
  47.4 1.0 fusion.26
  48.4 1.9 fusion.41
  50.3 0.8 convert_bitcast_fusion.3
  51.1 0.8 copy.115
  51.9 0.2 copy.93
  52.1 0.2 copy.86
  52.5 6.2 %add_bitcast_fusion.1 = f32[2,256,8,128]{1,3,2,0:T(8,128)} fusion(f32[2,8,128,256]{3,2,1,0:T(8,128)} %fusion.41, f32[2,64,8,128]{3,2,1,0:T(8,128)} %bitcast.173, f32[8]{0:T(128)S(1)} %copy-done.14, pred[2]{0:T(512)(128)(4,1)S(1)} %copy-done.16, f32[2,8,64]{2,1,0:T(8,128)S(1)} %get-tuple-element.30, f32[2,8,64,256]{3,2,1,0:T(8,128)} %copy-done.3), kind=kOutput, calls=%fused_computation.18 | convolution fusion | flops 68814080 | bytes 5771298 | tf_op jit(solution)/shard_map/bhrm,brhd->bmhd/dot_general | solution.py:21
  58.6 1.4 fusion.21
  60.0 0.9 fusion.67
  60.9 2.8 %multiply_reduce_fusion.3 = (f32[8]{0:T(128)S(1)}, f32[64,8]{0,1:T(8,128)S(1)}, f32[1,64,8,128]{3,1,2,0:T(8,128)}) fusion(f32[1,64,8,128]{3,2,1,0:T(8,128)S(1)} %bitcast.179, f32[8]{0:T(128)S(1)} %copy-done.14, pred[]{:T(512)S(6)} %and.13, bf16[256,8,128]{2,0,1:T(8,128)(2,1)} %collective-permute-done, f32[8,64]{1,0:T(8,128)S(1)} %get-tuple-element.32, ...), kind=kOutput, calls=%fused_computation.82 | convolution fusion | flops 34406648 | bytes 1577025 | tf_op jit(solution)/shard_map/bhrm,bmhd->brhd/dot_general | solution.py:21
  63.7 1.6 fusion.24
  65.3 1.3 fusion.45
  66.7 3.4 %fusion.17 = bf16[256,8,128]{0,2,1:T(8,128)(2,1)} fusion(f32[8,128,256]{2,1,0:T(8,128)} %fusion.45, f32[8,8,8,128]{3,2,1,0:T(8,128)} %get-tuple-element.24, f32[8]{0:T(128)S(1)} %copy-done.14, pred[]{:T(512)S(6)} %and.13, f32[8,64]{1,0:T(8,128)S(1)} %get-tuple-element.32, f32[8,64,256]{2,1,0:T(8,128)S(1)} %fusion.21), kind=kOutput, calls=%fused_computation.34 | convolution fusion | flops 34669312 | bytes 2361377 | tf_op jit(solution)/shard_map/bhrm,brhd->bmhd/dot_general | solution.py:21
  70.1 1.3 collective-permute-start.1
  71.4 16.4 %psum.30 = f32[8]{0:T(128)S(1)} all-reduce(f32[8]{0:T(128)S(1)} %add.81), channel_id=1, replica_groups=mesh['group'=4,'dp'=32,'tensor'=4] {'group'}, use_global_device_ids=true, to_apply=%region_15.16 | all-reduce | flops 8 | bytes 64 | tf_op jit(solution)/shard_map/psum | solution.py:155
  87.7 1.1 fusion.40
  88.8 70.7 %psum.31 = f32[8]{0:T(128)S(1)} all-reduce(f32[8]{0:T(128)S(1)} %psum.30), channel_id=1, replica_groups=mesh['group'=4,'dp'=32,'tensor'=4] {'dp'}, use_global_device_ids=true, to_apply=%region_16.17 | all-reduce | flops 8 | bytes 64 | tf_op jit(solution)/shard_map/psum | solution.py:155
  159.5 0.1 copy.182
  159.6 1.3 fusion.27
  160.9 0.1 copy.181
  161.1 0.9 pad_maximum_fusion.5
  162.0 0.5 multiply_multiply_fusion
  162.5 2.3 %fusion.28 = f32[2,256,8,128]{1,3,2,0:T(8,128)} fusion(f32[2,256,8,128]{1,3,2,0:T(8,128)} %add_bitcast_fusion.1, bf16[256,8,128]{0,2,1:T(8,128)(2,1)S(1)} %collective-permute-done.1), kind=kLoop, calls=%fused_computation.54 | loop fusion | flops 524288 | bytes 2621440 | tf_op jit(solution)/shard_map/scatter-add | solution.py:136
  164.9 3.0 %copy.96 = f32[2,256,8,128]{3,2,1,0:T(8,128)} copy(f32[2,256,8,128]{1,3,2,0:T(8,128)} %fusion.28) | data formatting | bytes 4194304 | tf_op jit(solution)/shard_map/scatter-add | solution.py:136
  167.9 1.9 convert_element_type.156
  169.8 0.3 copy-done
  170.1 2.3 %fusion.7 = f32[2,2,128,8]{2,3,1,0:T(8,128)S(1)} fusion(f32[2,2,8,128,128]{3,4,2,1,0:T(8,128)} %get-tuple-element.29, f32[2,2,128,8,128]{4,3,2,1,0:T(8,128)S(1)} %bitcast.153), kind=kLoop, calls=%fused_computation.15 | loop fusion | flops 1044480 | bytes 4210688 | tf_op jit(solution)/shard_map/reduce_sum | solution.py:43
  172.5 1.2 multiply_convert_fusion
  173.7 0.6 fusion.68
  174.2 0.9 add_bitcast_fusion
  175.1 2.6 %multiply_reduce_fusion = (f32[2,2,128]{2,1,0:T(2,128)S(1)}, f32[2,2,128,8,128]{4,2,3,1,0:T(8,128)}) fusion(f32[2,2,128,8,128]{4,3,2,1,0:T(8,128)S(1)} %bitcast.149, f32[2,2,128]{2,1,0:T(2,128)S(1)} %add_rsqrt_fusion, f32[8,128]{1,0:T(8,128)S(1)} %bitcast.182, f32[2,2,192,8,128]{4,2,3,1,0:T(8,128)S(1)} %add_bitcast_fusion, ...), kind=kOutput, calls=%fused_computation.17 | convolution fusion | flops 207093248 | bytes 9445376 | tf_op jit(solution)/shard_map/cjhqk,cjkhd->cjqhd/dot_general | solution.py:21
  177.8 0.2 copy.100
  177.9 0.8 copy.178
  178.7 10.1 %psum.29 = f32[2,2,128]{2,1,0:T(2,128)S(1)} all-reduce(f32[2,2,128]{2,1,0:T(2,128)S(1)} %get-tuple-element.35), channel_id=1, replica_groups=mesh['group'=4,'dp'=32,'tensor'=4] {'tensor'}, use_global_device_ids=true, to_apply=%region_12.13 | all-reduce | flops 512 | bytes 4096 | tf_op jit(solution)/shard_map/psum | solution.py:152
  188.8 3.1 %add_convert_fusion = bf16[2,2,128,8,128]{4,2,3,1,0:T(8,128)(2,1)S(1)} fusion(f32[2,2,128,8,128]{4,2,3,1,0:T(8,128)} %get-tuple-element.36, f32[2,2,128,8,128]{4,3,2,1,0:T(8,128)} %bitcast.152, f32[2,2,128,8,128]{4,3,2,1,0:T(8,128)S(1)} %bitcast.150, f32[2,2,128]{2,1,0:T(2,128)S(1)} %broadcast_multiply_fusion, f32[2,2,128]{2,1,0:T(2,128)S(1)} %add_rsqrt_fusion), kind=kLoop, calls=%fused_computation.16 | loop fusion | flops 3145728 | bytes 7344128 | tf_op jit(solution)/shard_map/convert_element_type | solution.py:161
  191.9 0.7 copy.103
  192.6 1.3 copy.177
  (73 shorter events, 0.8 us)
Async XLA Ops:
  0.6 18.0 %copy-start.10 = (bf16[128,1024]{1,0:T(8,128)(2,1)S(1)}, bf16[128,1024]{1,0:T(8,128)(2,1)}, u32[]{:S(2)}) copy-start(bf16[128,1024]{1,0:T(8,128)(2,1)} %param.10) | copy-start | bytes 786436
  18.7 2.1 %copy-start.13 = (f32[1024]{0:T(1024)S(1)}, f32[1024]{0:T(1024)}, u32[]{:S(2)}) copy-start(f32[1024]{0:T(1024)} %param.13) | copy-start | bytes 12292
  21.4 1.0 copy-start.1
  21.5 1.0 copy-start.5
  22.4 2.6 %copy-start.21 = (f32[2,2,8,128,192]{3,4,2,1,0:T(8,128)}, f32[2,2,8,128,192]{3,4,2,1,0:T(8,128)S(1)}, u32[]{:S(2)}) copy-start(f32[2,2,8,128,192]{3,4,2,1,0:T(8,128)S(1)} %get-tuple-element.27) | copy-start | bytes 9437188
  22.4 2.6 %copy-start.23 = (f32[2,2,8,128]{3,2,1,0:T(8,128)}, f32[2,2,8,128]{3,2,1,0:T(8,128)S(1)}, u32[]{:S(2)}) copy-start(f32[2,2,8,128]{3,2,1,0:T(8,128)S(1)} %get-tuple-element.26) | copy-start | bytes 49156
  24.9 1.0 copy-start.4
  24.9 4.4 %copy-start.15 = (s32[1,64]{1,0:T(1,128)S(1)}, s32[1,64]{1,0:T(1,128)}, u32[]{:S(2)}) copy-start(s32[1,64]{1,0:T(1,128)} %param.12) | copy-start | bytes 772
  24.9 6.8 %copy-start.9 = (bf16[128,1024]{1,0:T(8,128)(2,1)S(1)}, bf16[128,1024]{1,0:T(8,128)(2,1)}, u32[]{:S(2)}) copy-start(bf16[128,1024]{1,0:T(8,128)(2,1)} %param.9) | copy-start | bytes 786436
  25.0 6.9 %copy-start.8 = (bf16[128,1024]{1,0:T(8,128)(2,1)S(1)}, bf16[128,1024]{1,0:T(8,128)(2,1)}, u32[]{:S(2)}) copy-start(bf16[128,1024]{1,0:T(8,128)(2,1)} %param.15) | copy-start | bytes 786436
  26.3 8.2 %copy-start.17 = (f32[8]{0:T(128)S(1)}, f32[8]{0:T(128)}, u32[]{:S(2)}) copy-start(f32[8]{0:T(128)} %param.14) | copy-start | bytes 100
  27.2 31.4 %collective-permute-start = (bf16[256,8,128]{2,0,1:T(8,128)(2,1)}, bf16[256,8,128]{2,0,1:T(8,128)(2,1)}, u32[]{:S(2)}, u32[]{:S(2)}) collective-permute-start(bf16[256,8,128]{2,0,1:T(8,128)(2,1)} %copy.79), channel_id=1, source_target_pairs={{0,4},{4,8},{8,12},{12,16},{16,20},{20,24},{24,28},{28,32},{32,36}... | collective-permute-start | bytes 1572872 | tf_op jit(solution)/shard_map/ppermute | solution.py:17
  38.2 1.0 copy-start.3
  48.4 1.9 slice-start
  48.4 3.4 %copy-start.7 = (bf16[2,64,8,128]{3,1,2,0:T(8,128)(2,1)S(1)}, bf16[2,64,8,128]{3,1,2,0:T(8,128)(2,1)}, u32[]{:S(2)}) copy-start(bf16[2,64,8,128]{3,1,2,0:T(8,128)(2,1)} %fusion.26) | copy-start | bytes 786436
  50.3 1.8 copy-start.12
  50.3 2.1 %copy-start.20 = (pred[2]{0:T(512)(128)(4,1)S(1)}, pred[2]{0:T(512)(128)(4,1)}, u32[]{:S(2)}) copy-start(pred[2]{0:T(512)(128)(4,1)} %iota_compare_fusion.1) | copy-start | bytes 10
  50.3 2.1 %copy-start.14 = (f32[8]{0:T(128)S(1)}, f32[8]{0:T(128)}, u32[]{:S(2)}) copy-start(f32[8]{0:T(128)} %tanh.3) | copy-start | bytes 100
  50.3 2.1 %copy-start.16 = (pred[2]{0:T(512)(128)(4,1)S(1)}, pred[2]{0:T(512)(128)(4,1)}, u32[]{:S(2)}) copy-start(pred[2]{0:T(512)(128)(4,1)} %get-tuple-element.21) | copy-start | bytes 10
  58.6 2.3 %copy-start.11 = (f32[8,8,8,128]{3,2,1,0:T(8,128)S(1)}, f32[8,8,8,128]{3,2,1,0:T(8,128)}, u32[]{:S(2)}) copy-start(f32[8,8,8,128]{3,2,1,0:T(8,128)} %copy.115) | copy-start | bytes 786436
  65.3 4.7 %copy-start.19 = (f32[8]{0:T(128)S(1)}, f32[8]{0:T(128)}, u32[]{:S(2)}) copy-start(f32[8]{0:T(128)} %get-tuple-element.17) | copy-start | bytes 100
  70.1 92.5 %collective-permute-start.1 = (bf16[256,8,128]{0,2,1:T(8,128)(2,1)}, bf16[256,8,128]{0,2,1:T(8,128)(2,1)S(1)}, u32[]{:S(2)}, u32[]{:S(2)}) collective-permute-start(bf16[256,8,128]{0,2,1:T(8,128)(2,1)} %fusion.17), channel_id=1, source_target_pairs={{4,0},{8,4},{12,8},{16,12},{20,16},{24,20},{28,24},{32,28},{36,32}... | collective-permute-start | bytes 1572872 | tf_op jit(solution)/shard_map/ppermute | solution.py:17
  87.7 74.3 %copy-start.18 = (f32[8]{0:T(128)S(1)}, f32[8]{0:T(128)}, u32[]{:S(2)}) copy-start(f32[8]{0:T(128)} %param.14) | copy-start | bytes 100
  167.9 2.2 %copy-start = (f32[2,256,8,128]{3,2,1,0:T(8,128)S(1)}, f32[2,256,8,128]{3,2,1,0:T(8,128)}, u32[]{:S(2)}) copy-start(f32[2,256,8,128]{3,2,1,0:T(8,128)} %copy.96) | copy-start | bytes 6291460
  167.9 4.6 %copy-start.22 = (f32[2,2,8,128,192]{3,4,2,1,0:T(8,128)S(1)}, f32[2,2,8,128,192]{3,4,2,1,0:T(8,128)}, u32[]{:S(2)}) copy-start(f32[2,2,8,128,192]{3,4,2,1,0:T(8,128)} %copy-done.21) | copy-start | bytes 9437188
  170.1 2.3 %copy-start.2 = (bf16[2,2,128,8,128]{4,2,3,1,0:T(8,128)(2,1)S(1)}, bf16[2,2,128,8,128]{4,2,3,1,0:T(8,128)(2,1)}, u32[]{:S(2)}) copy-start(bf16[2,2,128,8,128]{4,2,3,1,0:T(8,128)(2,1)} %copy-done.1) | copy-start | bytes 3145732
  170.1 2.4 %copy-start.6 = (bf16[2,2,64,8,128]{4,2,3,1,0:T(8,128)(2,1)S(1)}, bf16[2,2,64,8,128]{4,2,3,1,0:T(8,128)(2,1)}, u32[]{:S(2)}) copy-start(bf16[2,2,64,8,128]{4,2,3,1,0:T(8,128)(2,1)} %copy-done.5) | copy-start | bytes 1572868
  170.1 2.4 %copy-start.24 = (f32[2,2,8,128]{3,2,1,0:T(8,128)S(1)}, f32[2,2,8,128]{3,2,1,0:T(8,128)}, u32[]{:S(2)}) copy-start(f32[2,2,8,128]{3,2,1,0:T(8,128)} %copy-done.23) | copy-start | bytes 49156
